TPU v7x, 256 devices: a whole 4x4x8 slice. The times are simulated.
256 devices in a mesh: prow: 16 (over z, x_hi), pcol: 16 (over x_lo, y, core).
Axes of the slice: x: 4 (x_hi: 2, x_lo: 2; x = x_hi * 2 + x_lo), y: 4, z: 8, core: 2. Of those that a mesh axis runs over, the one named last changes fastest.
Arguments:
- sigma_anc: float32 [6144, 6144], P('prow', 'pcol')
- panels: float32 [16384, 6144], P('pcol', 'prow'), may hold values from -0.8 to 0.8
- diag_blocks: float32 [32, 512, 512], P('pcol', 'prow'), may hold values from -6 to 6
- anc_blocks: int32 [32, 6], replicated, may hold values from 0 to 15, as said below
Outputs:
- cross_panel: float32 [16384, 6144], P('pcol', 'prow')
- diag_out: float32 [32, 512, 512], P('pcol', 'prow')
Inputs may be any that keep to these rules, and one draw needn't show every extreme that they name: `anc_blocks`: each row holds 6 distinct block numbers.
All inputs are finite; a program needn't handle non-finite values.
Results may differ from a plain program's by a relative error of at most 0.000075.
Values sent between devices are 32-bit elements; how exact they have to be, the bound alone decides.
A program may use at most 128 MiB of HBM per device.

v0:
```python
import jax
import jax.numpy as jnp
from jax import lax
from jax.sharding import PartitionSpec as P

W = 512
BLK = 384


def local(sigma_anc, panels, diag_blocks, anc_blocks):
    local_rows = panels.shape[0]
    slab_cols = panels.shape[1]
    groups = local_rows // W
    block_count = slab_cols // BLK
    row_index = lax.axis_index("prow")
    col_index = lax.axis_index("pcol")
    blocks = row_index * block_count + jnp.arange(block_count, dtype=jnp.int32)
    member = jnp.any(anc_blocks[:, :, None] == blocks[None, None, :], axis=1).astype(jnp.float32)
    owned = lax.dynamic_slice_in_dim(member, col_index * groups, groups, 0)
    rowmask = jnp.repeat(jnp.repeat(owned, W, axis=0), BLK, axis=1)
    masked = panels * rowmask
    whole_rows = lax.all_gather(masked, "prow", axis=1, tiled=True)
    image = jnp.dot(
        whole_rows,
        lax.all_gather(sigma_anc, "pcol", axis=1, tiled=True).T,
        precision=lax.Precision.HIGHEST,
    )
    image = image * rowmask
    left_cube = masked.reshape(groups, W, slab_cols)
    right_cube = image.reshape(groups, W, slab_cols)
    local_term = jnp.einsum("swr,svr->swv", left_cube, right_cube, precision=lax.Precision.HIGHEST)
    summed = lax.psum_scatter(local_term, "prow", scatter_dimension=1, tiled=True)
    return (-image, diag_blocks + summed)


def solution(mesh):
    placed = (P("prow", "pcol"), P("pcol", "prow"), P("pcol", "prow", None), P())
    return jax.shard_map(
        local,
        mesh=mesh,
        in_specs=placed,
        out_specs=(P("pcol", "prow"), P("pcol", "prow", None)),
        check_vma=False,
    )
```

profile of v0, /device:TPU:8, one launch (start us, length us, event | category | flops | bytes accessed | tf_op | source)
XLA Modules:
  0.0 652.5 jit_solution(8713940888428418367)
XLA Ops:
  7.2 0.0 all-gather.5.cloned.1.call-start
  7.2 0.7 all-gather.5.cloned.1.call-update
  7.9 0.0 all-gather.3.cloned.1.call-start
  7.9 0.7 compare_reduce_fusion
  8.7 0.1 dynamic-slice.3
  8.7 0.1 broadcast_bitcast_fusion
  8.8 2.7 broadcast_multiply_fusion
  11.6 0.0 all-gather.3.cloned.1.call-update
  11.6 0.0 copy-start
  11.6 0.0 reduce-scatter.2.cloned.1.call-start
  11.6 60.7 %all-gather.5.cloned.1.call-done = f32[384,6144]{1,0:T(8,128)} async-done(((f32[384,384]{1,0:T(8,128)}), f32[384,6144]{1,0:T(8,128)}) %all-gather.5.cloned.1.call-update) | async-done | bytes 9437200 | tf_op jit(solution)/shard_map/all_gather | solution.py:25
  72.3 322.0 %all-gather.3.cloned.1.call-done = f32[1024,6144]{1,0:T(8,128)} async-done(((f32[1024,384]{1,0:T(8,128)}), f32[1024,6144]{1,0:T(8,128)}) %all-gather.3.cloned.1.call-update) | async-done | bytes 25165840 | tf_op jit(solution)/shard_map/all_gather | solution.py:22
  394.3 44.1 %fusion = (f32[1024,384]{1,0:T(8,128)}, f32[1024,384]{1,0:T(8,128)S(1)}) fusion(f32[1024]{0:T(1024)S(1)} %bitcast.12, f32[1024,6144]{1,0:T(8,128)} %all-gather.3.cloned.1.call-done, f32[384,6144]{1,0:T(8,128)} %all-gather.5.cloned.1.call-done), kind=kOutput, calls=%fused_computation.4 | convolution fusion | flops 28991815680 | bytes 37752832 | tf_op jit(solution)/shard_map/dot_general | solution.py:23
  438.4 0.0 copy-done
  438.4 4.8 fusion.1
  443.3 0.0 copy-start.1
  443.3 0.0 reduce-scatter.2.cloned.1.call-update
  443.3 201.1 %reduce-scatter.2.cloned.1.call-done = f32[2,32,512]{2,1,0:T(8,128)} async-done(((f32[2,512,512]{2,1,0:T(8,128)}), f32[2,32,512]{2,1,0:T(8,128)}) %reduce-scatter.2.cloned.1.call-update) | async-done | bytes 131088 | tf_op jit(solution)/shard_map/reduce_scatter | solution.py:32
  644.4 0.0 copy-done.1
  644.4 1.6 add.9
  (2 shorter events, 0.0 us)
Async XLA Ops:
  7.2 65.2 %all-gather.5.cloned.1.call-start = ((), (), s32[]{:S(2)}) async-start(), calls=%async_computation.2 | async-start | bytes 10027008 | tf_op jit(solution)/shard_map/all_gather | solution.py:25
  7.9 386.4 %all-gather.3.cloned.1.call-start = ((), (), s32[]{:S(2)}) async-start(), calls=%async_computation.1 | async-start | bytes 26738688 | tf_op jit(solution)/shard_map/all_gather | solution.py:22
  11.6 426.8 %copy-start = (f32[1024,384]{1,0:T(8,128)S(1)}, f32[1024,384]{1,0:T(8,128)}, u32[]{:S(2)}) copy-start(f32[1024,384]{1,0:T(8,128)} %broadcast_multiply_fusion) | copy-start | bytes 4718596
  11.6 632.8 %reduce-scatter.2.cloned.1.call-start = ((), (), s32[]{:S(2)}) async-start(), calls=%async_computation.3 | async-start | bytes 2228224 | tf_op jit(solution)/shard_map/reduce_scatter | solution.py:32
  443.3 201.1 %copy-start.1 = (f32[2,32,512]{2,1,0:T(8,128)S(1)}, f32[2,32,512]{2,1,0:T(8,128)}, u32[]{:S(2)}) copy-start(f32[2,32,512]{2,1,0:T(8,128)} %param.6) | copy-start | bytes 393220
Sparse Core Ops, SparseCore 0:
  9.8 62.4 all-gather.4
  75.0 319.3 all-gather.2
  443.4 200.9 reduce-scatter.1
where the time goes:
time: 653 us; the launch traced here: 652 us
  waiting for transfers between devices  584 us (89%)
  matrix products  48.9 us (7%)
  between operations  13.8 us (2%)
    all_gather x1, waiting for transfers between devices, local(): whole_rows = lax.all_gather(masked, 'prow', axis=1, tiled=True)  322 us
    reduce_scatter x1, waiting for transfers between devices, local(): lax.psum_scatter(local_term, 'prow', scatter_dimension=1, tiled=True)  201 us
    all_gather x1, waiting for transfers between devices, local(): lax.all_gather(sigma_anc, 'pcol', axis=1, tiled=True)  60.7 us
    dot_general x1, matrix products, local(): jnp.dot(whole_rows, lax.all_gather(sigma_anc, 'pcol', axis=1, tiled=True)...  44.1 us
  transfers between devices with their start and end apart: 3, of which 3 were waited for; matrix products, arithmetic and copies ran while one was open for 1% of the time, Pallas kernels for 0%

commit v1 on v0

v1 whole, which is shorter than its diff:
```python
import functools

import jax
import jax.numpy as jnp
from jax import lax
from jax.experimental import pallas as pl
from jax.experimental.pallas import tpu as pltpu
from jax.sharding import PartitionSpec as P

W = 512
BLK = 384
NB = 16
K = 6
MESH = pl.DeviceIdType.MESH
F32 = jnp.float32
BF16 = jnp.bfloat16


def split(value):
    high = value.astype(BF16)
    return high, (value - high.astype(F32)).astype(BF16)


def kernel(
    anc, sig, pan, diag, cross, dout,
    abuf0, abuf1, pf0, pf1, sbuf, shi, slo, cacc, dbuf, drx, ebuf, drz,
    a_s, a_r, z_s, z_r, x_s, x_r, y_s, y_r, c_s, c_r, d_s, d_r, e_s, e_r,
):
    row, col = lax.axis_index("prow"), lax.axis_index("pcol")
    z, xh = row // 2, row % 2
    xl, y, core = col // 8, (col // 2) % 4, col % 2
    abuf, pf = (abuf0, abuf1), (pf0, pf1)

    def at_row(zz, xx):
        return (zz * 2 + xx, col)

    def at_col(ll, yy, cc):
        return (row, (ll * 4 + yy) * 2 + cc)

    def colnum(ll, yy, cc):
        return (ll * 4 + yy) * 2 + cc

    z_next = (at_row((z + 1) % 8, xh), at_row((z + 7) % 8, xh))
    x_pair = at_row(z, 1 - xh)
    l_pair = at_col(1 - xl, y, core)
    y_next = (at_col(xl, (y + 1) % 4, core), at_col(xl, (y + 3) % 4, core))
    c_pair = at_col(xl, y, 1 - core)
    row_peers = [((row + i) % 16, col) for i in range(1, 16)]

    barrier = pltpu.get_barrier_semaphore()
    peers = row_peers + [l_pair, *y_next, c_pair]
    for peer in peers:
        pl.semaphore_signal(barrier, inc=1, device_id=peer, device_id_type=MESH)
    pl.semaphore_wait(barrier, len(peers))

    sent = []

    def send(src, dst, ssem, rsem, peer):
        copy = pltpu.make_async_remote_copy(
            src_ref=src, dst_ref=dst, send_sem=ssem, recv_sem=rsem,
            device_id=peer, device_id_type=MESH,
        )
        copy.start()
        sent.append(copy)

    def arrived(dst, ssem, rsem, peer):
        pltpu.make_async_remote_copy(
            src_ref=dst, dst_ref=dst, send_sem=ssem, recv_sem=rsem,
            device_id=peer, device_id_type=MESH,
        ).wait_recv()

    for s in range(2):
        for i in range(1, 16):
            peer = (row + i) % 16
            send(pan.at[s, peer], abuf[s].at[row], a_s.at[s, i], a_r.at[s, i], (peer, col))
        abuf[s][pl.ds(row, 1)] = pan[s, pl.ds(row, 1)]

    sbuf[pl.ds(col, 1)] = sig[...].T[None]
    mine, pair = sbuf.at[col], sbuf.at[colnum(1 - xl, y, core)]
    send(mine, mine, y_s.at[6], y_r.at[6], l_pair)
    for d in range(2):
        send(mine, mine, y_s.at[d], y_r.at[d], y_next[d])
    send(mine, mine, c_s.at[0], c_r.at[0], c_pair)

    def sigma_pair():
        arrived(pair, y_s.at[6], y_r.at[6], l_pair)
        for d in range(2):
            send(pair, pair, y_s.at[2 + d], y_r.at[2 + d], y_next[d])
        send(pair, pair, c_s.at[1], c_r.at[1], c_pair)

    def sigma_near():
        for t in range(2):
            for d in range(2):
                block = sbuf.at[colnum(xl if t == 0 else 1 - xl, (y + (3 if d == 0 else 1)) % 4, core)]
                arrived(block, y_s.at[2 * t + d], y_r.at[2 * t + d], y_next[d])
                if t == d:
                    send(block, block, y_s.at[4 + t], y_r.at[4 + t], y_next[d])
                i = 2 + 2 * t + d
                send(block, block, c_s.at[i], c_r.at[i], c_pair)

    def sigma_far():
        for t in range(2):
            block = sbuf.at[colnum(xl if t == 0 else 1 - xl, (y + 2) % 4, core)]
            arrived(block, y_s.at[4 + t], y_r.at[4 + t], y_next[t])
            send(block, block, c_s.at[6 + t], c_r.at[6 + t], c_pair)

    def sigma_other_core():
        for i in range(8):
            t, yy = (
                (0, y), (1, y), (0, (y + 3) % 4), (0, (y + 1) % 4),
                (1, (y + 3) % 4), (1, (y + 1) % 4), (0, (y + 2) % 4), (1, (y + 2) % 4),
            )[i]
            block = sbuf.at[colnum(xl if t == 0 else 1 - xl, yy, 1 - core)]
            arrived(block, c_s.at[i], c_r.at[i], c_pair)

        def cut(i, carry):
            high, low = split(sbuf[i])
            shi[i] = high
            slo[i] = low
            return carry

        lax.fori_loop(0, NB, cut, 0)

    def compact(s):
        for i in range(1, 16):
            peer = (row + 16 - i) % 16
            arrived(abuf[s].at[peer], a_s.at[s, i], a_r.at[s, i], (peer, col))

        def take(k, carry):
            block = anc[2 * col + s, k]
            rows = abuf[s][block].reshape(2, 16, BLK)
            pf[s][0, pl.ds(row, 1), k] = rows[0][None]
            pf[s][1, pl.ds(row, 1), k] = rows[1][None]
            return carry

        lax.fori_loop(0, K, take, 0)

    def hops(s, kind, d):
        long = (s + (1 if kind == 2 else 0)) % 2
        return 4 if d == long else 3

    def piece(s, kind, zz):
        return pf[s].at[1 if kind == 1 else 0, zz * 2 + (1 - xh if kind == 2 else xh)]

    def z_send(s, kind, d, hop):
        block = piece(s, kind, (z + (8 - hop if d == 0 else hop)) % 8)
        send(block, block, z_s.at[s, kind, d, hop], z_r.at[s, kind, d, hop], z_next[d])

    def x_send(s, i, block):
        send(block, block, x_s.at[s, i], x_r.at[s, i], x_pair)

    def gather_start(s):
        x_send(s, 8, piece(s, 0, z))
        for kind in (0, 1):
            for d in range(2):
                z_send(s, kind, d, 0)
        x_send(s, 0, piece(s, 1, z))

    def gather_pair(s):
        arrived(piece(s, 2, z), x_s.at[s, 8], x_r.at[s, 8], x_pair)
        for d in range(2):
            z_send(s, 2, d, 0)

    def gather_hop(s, kind, hop):
        for d in range(2):
            if hop > hops(s, kind, d):
                continue
            block = piece(s, kind, (z + (8 - hop if d == 0 else hop)) % 8)
            arrived(block, z_s.at[s, kind, d, hop - 1], z_r.at[s, kind, d, hop - 1], z_next[d])
            if hop < hops(s, kind, d):
                z_send(s, kind, d, hop)
            if kind == 1:
                x_send(s, hop if d == 0 else 8 - hop, block)

    def gather_x(s):
        for i in range(8):
            block = pf[s].at[1, ((z + 8 - i) % 8) * 2 + 1 - xh]
            arrived(block, x_s.at[s, i], x_r.at[s, i], x_pair)

    def member(s):
        here = jnp.int32(0)
        for k in range(K):
            here = here + (anc[2 * col + s, k] == row).astype(jnp.int32)
        return here.astype(F32)

    def image(s, h):
        keep = member(s)
        cacc[...] = jnp.zeros_like(cacc)

        def term(k, carry):
            block = anc[2 * col + s, k]
            high, low = split(pf[s][h, :, k].reshape(256, BLK))
            s_high, s_low = shi[block], slo[block]
            cacc[...] += (
                jnp.dot(high, s_high, preferred_element_type=F32)
                + jnp.dot(low, s_high, preferred_element_type=F32)
                + jnp.dot(high, s_low, preferred_element_type=F32)
            )
            return carry

        lax.fori_loop(0, K, term, 0)
        rows = cacc[...] * keep
        cross[s, :, h] = -rows.reshape(16, 16, BLK)
        c_high, c_low = split(rows)
        p_high, p_low = split(pan[s].reshape(W, BLK) * keep)
        over = (((1,), (1,)), ((), ()))
        product = (
            lax.dot_general(c_high, p_high, over, preferred_element_type=F32)
            + lax.dot_general(c_low, p_high, over, preferred_element_type=F32)
            + lax.dot_general(c_high, p_low, over, preferred_element_type=F32)
        )
        dbuf[s, h] = product.reshape(8, 2, 16, W)
        send(dbuf.at[s, h, :, 1 - xh], drx.at[s, h], d_s.at[s, h], d_r.at[s, h], x_pair)

    def diag_z(s, h):
        arrived(drx.at[s, h], d_s.at[s, h], d_r.at[s, h], x_pair)
        ebuf[s, h] = dbuf[s, h, :, pl.ds(xh, 1)].reshape(8, 16, W) + drx[s, h]
        for i in range(1, 8):
            zz = (z + i) % 8
            send(ebuf.at[s, h, zz], drz.at[s, h, i], e_s.at[s, h, i], e_r.at[s, h, i], at_row(zz, xh))

    def diag_end(s, h):
        total = diag[s, h] + ebuf[s, h, pl.ds(z, 1)].reshape(16, W)
        for i in range(1, 8):
            arrived(drz.at[s, h, i], e_s.at[s, h, i], e_r.at[s, h, i], at_row((z + 8 - i) % 8, xh))
            total = total + drz[s, h, i]
        dout[s, h] = total

    sigma_pair()
    compact(0)
    gather_start(0)
    sigma_near()
    gather_pair(0)
    compact(1)
    for kind in (0, 1, 2):
        gather_hop(0, kind, 1)
    gather_start(1)
    sigma_far()
    for kind in (0, 1, 2):
        gather_hop(0, kind, 2)
    gather_pair(1)
    for hop in (3, 4):
        for kind in (0, 1, 2):
            gather_hop(0, kind, hop)
    sigma_other_core()
    for kind in (0, 1, 2):
        gather_hop(1, kind, 1)
    image(0, 0)
    for kind in (0, 1, 2):
        gather_hop(1, kind, 2)
    gather_x(0)
    image(0, 1)
    for kind in (0, 1, 2):
        gather_hop(1, kind, 3)
    diag_z(0, 0)
    diag_z(0, 1)
    for kind in (0, 1, 2):
        gather_hop(1, kind, 4)
    image(1, 0)
    gather_x(1)
    image(1, 1)
    diag_end(0, 0)
    diag_end(0, 1)
    diag_z(1, 0)
    diag_z(1, 1)
    diag_end(1, 0)
    diag_end(1, 1)
    for copy in sent:
        copy.wait_send()


def local(sigma_anc, panels, diag_blocks, anc_blocks):
    vmem = pl.BlockSpec(memory_space=pltpu.VMEM)
    dma = pltpu.SemaphoreType.DMA
    cross, dout = pl.pallas_call(
        kernel,
        out_shape=(
            jax.ShapeDtypeStruct((2, 16, 2, 16, BLK), F32),
            jax.ShapeDtypeStruct((2, 2, 16, W), F32),
        ),
        in_specs=[pl.BlockSpec(memory_space=pltpu.SMEM), vmem, vmem, vmem],
        out_specs=(vmem, vmem),
        scratch_shapes=[
            pltpu.VMEM((16, 32, BLK), F32),
            pltpu.VMEM((16, 32, BLK), F32),
            pltpu.VMEM((2, 16, K, 16, BLK), F32),
            pltpu.VMEM((2, 16, K, 16, BLK), F32),
            pltpu.VMEM((NB, BLK, BLK), F32),
            pltpu.VMEM((NB, BLK, BLK), BF16),
            pltpu.VMEM((NB, BLK, BLK), BF16),
            pltpu.VMEM((256, BLK), F32),
            pltpu.VMEM((2, 2, 8, 2, 16, W), F32),
            pltpu.VMEM((2, 2, 8, 16, W), F32),
            pltpu.VMEM((2, 2, 8, 16, W), F32),
            pltpu.VMEM((2, 2, 8, 16, W), F32),
            dma((2, 16)), dma((2, 16)),
            dma((2, 3, 2, 4)), dma((2, 3, 2, 4)),
            dma((2, 9)), dma((2, 9)),
            dma((7,)), dma((7,)),
            dma((8,)), dma((8,)),
            dma((2, 2)), dma((2, 2)),
            dma((2, 2, 8)), dma((2, 2, 8)),
        ],
        compiler_params=pltpu.CompilerParams(
            collective_id=0, has_side_effects=True, vmem_limit_bytes=56 << 20
        ),
    )(
        anc_blocks,
        sigma_anc,
        panels.reshape(2, 16, 32, BLK),
        diag_blocks.reshape(2, 2, 16, W),
    )
    return cross.reshape(2 * W, BLK), dout.reshape(2, 32, W)


def solution(mesh):
    placed = (P("prow", "pcol"), P("pcol", "prow"), P("pcol", "prow", None), P())
    return jax.shard_map(
        local,
        mesh=mesh,
        in_specs=placed,
        out_specs=(P("pcol", "prow"), P("pcol", "prow", None)),
        check_vma=False,
    )
```

time: 653 us -> 160 us (0.25)
  waiting for transfers between devices: 584 us -> 0 us
  Pallas kernels: 0 us -> 153 us
  matrix products: 48.9 us -> 0 us
  between operations: 13.8 us -> 0.65 us
    all_gather x2 -> x0, waiting for transfers between devices: 383 us -> none  [the longest x1 322 us: local(): whole_rows = lax.all_gather(masked, 'prow', axis=1, tiled=True)]
    reduce_scatter x1 -> x0, waiting for transfers between devices: 201 us -> none  [local(): lax.psum_scatter(local_term, 'prow', scatter_dimension=1, tiled=True)]
    pallas_call x0 -> x1, Pallas kernels: none -> 153 us  [local(): pl.pallas_call(kernel, out_shape=(jax.ShapeDtypeStruct((2, 16, 2, 16, BLK...]
    dot_general x2 -> x0, matrix products: 48.9 us -> none  [the longest x1 44.1 us: local(): jnp.dot(whole_rows, lax.all_gather(sigma_anc, 'pcol', axis=1, tiled=True)...]
  transfers between devices with their start and end apart: 3 -> 0, of which waited for: 3 -> 0; matrix products, arithmetic and copies ran while one was open for 1% -> 0% of each run, Pallas kernels for 0% -> 0%
where the time goes in v1:
time: 160 us; the launch traced here: 158 us
  Pallas kernels  153 us (96%)
  local copies, waits for them, and re-layouts  4.72 us (3%)
    pallas_call x1, Pallas kernels, local(): pl.pallas_call(kernel, out_shape=(jax.ShapeDtypeStruct((2, 16, 2, 16, BLK...  153 us
    unnamed x5, local copies, waits for them, and re-layouts  4.72 us

profile of v1, /device:TPU:8, one launch (start us, length us, event | category | flops | bytes accessed | tf_op | source)
XLA Modules:
  0.0 158.2 jit_solution(2498910829368725607)
XLA Ops:
  0.6 1.4 copy.6.anc
  2.0 152.9 %shard_map.59 = (f32[2,16,2,16,384]{4,3,2,1,0:T(8,128)}, f32[2,2,16,512]{3,2,1,0:T(8,128)}) custom-call(s32[32,6]{1,0:T(8,128)} %copy.6.anc, f32[384,384]{1,0:T(8,128)} %sig.1, f32[2,16,32,384]{3,2,1,0:T(8,128)} %bitcast.4, f32[2,2,16,512]{3,2,1,0:T(8,128)} %bitcast.6), custom_call_target="tpu_custom_call" | custom-call | tf_op jit(solution)/shard_map/pallas_call | solution.py:275
  154.9 0.0 copy-start
  154.9 2.7 %copy.9 = f32[1024,384]{1,0:T(8,128)} copy(f32[1024,384]{1,0:T(8,128)} %bitcast.5) | data formatting | bytes 3145728
  157.6 0.0 copy-done
  157.6 0.7 copy.10
Async XLA Ops:
  154.9 2.7 %copy-start = (f32[2,2,16,512]{3,2,1,0:T(8,128)S(1)}, f32[2,2,16,512]{3,2,1,0:T(8,128)}, u32[]{:S(2)}) copy-start(f32[2,2,16,512]{3,2,1,0:T(8,128)} %get-tuple-element.5) | copy-start | bytes 393220

commit v2 on v0

v2 whole, which is shorter than its diff:
```python
import jax
import jax.numpy as jnp
from jax import lax
from jax.experimental import pallas as pl
from jax.experimental.pallas import tpu as pltpu
from jax.sharding import PartitionSpec as P

W = 512
BLK = 384
NB = 16
K = 6
MESH = pl.DeviceIdType.MESH
F32 = jnp.float32
BF16 = jnp.bfloat16


def split(value):
    high = value.astype(BF16)
    return high, (value - high.astype(F32)).astype(BF16)


def kernel(
    anc, sig, pan, diag, cross, dout,
    abuf0, abuf1, pf0, pf1, sbuf, pbuf, cacc, cbuf, dbuf, drz,
    a_s, a_r, z_s, z_r, p_s, p_r, c_s, c_r, sx_s, sx_r, sy_s, sy_r, sc_s, sc_r, d_s, d_r,
):
    row, col = lax.axis_index("prow"), lax.axis_index("pcol")
    z, xh = row // 2, row % 2
    xl, y, core = col // 8, (col // 2) % 4, col % 2
    x = 2 * xh + xl
    abuf, pf = (abuf0, abuf1), (pf0, pf1)

    def at(xx, yy, zz, cc):
        return (zz * 2 + xx // 2, ((xx % 2) * 4 + yy) * 2 + cc)

    def sigma_block(xx, yy, cc):
        return sbuf.at[(xx // 2) * NB + ((xx % 2) * 4 + yy) * 2 + cc]

    x_next = (at((x + 1) % 4, y, z, core), at((x + 3) % 4, y, z, core))
    y_next = (at(x, (y + 1) % 4, z, core), at(x, (y + 3) % 4, z, core))
    z_next = (at(x, y, (z + 1) % 8, core), at(x, y, (z + 7) % 8, core))
    x_pair = at((x + 2) % 4, y, z, core)
    c_pair = at(x, y, z, 1 - core)

    sbuf[pl.ds(xh * NB + col, 1)] = sig[...].T[None]
    for s in range(2):
        abuf[s][pl.ds(row, 1)] = pan[s, pl.ds(row, 1)]

    barrier = pltpu.get_barrier_semaphore()
    peers = [((row + i) % 16, col) for i in range(1, 16)] + [*x_next, *y_next, c_pair]
    for peer in peers:
        pl.semaphore_signal(barrier, inc=1, device_id=peer, device_id_type=MESH)
    pl.semaphore_wait(barrier, len(peers))

    sent = []

    def send(src, dst, ssem, rsem, peer):
        copy = pltpu.make_async_remote_copy(
            src_ref=src, dst_ref=dst, send_sem=ssem, recv_sem=rsem,
            device_id=peer, device_id_type=MESH,
        )
        copy.start()
        sent.append(copy)

    def arrived(dst, ssem, rsem, peer):
        pltpu.make_async_remote_copy(
            src_ref=dst, dst_ref=dst, send_sem=ssem, recv_sem=rsem,
            device_id=peer, device_id_type=MESH,
        ).wait_recv()

    steps = (0, 3, 1, 2)

    def sigma_at(t, u, cc):
        return sigma_block((x + steps[t]) % 4, (y + steps[u]) % 4, cc)

    def sigma_core(t, u):
        block = sigma_at(t, u, core)
        send(block, block, sc_s.at[t, u], sc_r.at[t, u], c_pair)

    def sigma_y(t):
        block = sigma_at(t, 0, core)
        for d in range(2):
            send(block, block, sy_s.at[t, d], sy_r.at[t, d], y_next[d])

    def sigma_own():
        block = sigma_at(0, 0, core)
        for d in range(2):
            send(block, block, sx_s.at[d], sx_r.at[d], x_next[d])
        sigma_y(0)
        sigma_core(0, 0)

    def sigma_x_near():
        for d in range(2):
            block = sigma_at(1 + d, 0, core)
            arrived(block, sx_s.at[d], sx_r.at[d], x_next[d])

            @pl.when(core == d)
            def _():
                pltpu.make_async_remote_copy(
                    src_ref=block, dst_ref=block, send_sem=sx_s.at[2], recv_sem=sx_r.at[2],
                    device_id=x_next[d], device_id_type=MESH,
                ).start()

            sigma_y(1 + d)
            sigma_core(1 + d, 0)

    def sigma_x_far():
        block = sigma_at(3, 0, core)
        arrived(block, sx_s.at[2], sx_r.at[2], x_pair)
        sigma_y(3)
        sigma_core(3, 0)

    def sigma_y_near(t):
        for d in range(2):
            block = sigma_at(t, 1 + d, core)
            arrived(block, sy_s.at[t, d], sy_r.at[t, d], y_next[d])
            if d == t % 2:
                send(block, block, sy_s.at[t, 2], sy_r.at[t, 2], y_next[d])
            sigma_core(t, 1 + d)

    def sigma_y_far(t):
        block = sigma_at(t, 3, core)
        arrived(block, sy_s.at[t, 2], sy_r.at[t, 2], y_next[t % 2])
        sigma_core(t, 3)

    def sigma_other_core():
        for t in range(4):
            for u in range(4):
                arrived(sigma_at(t, u, 1 - core), sc_s.at[t, u], sc_r.at[t, u], c_pair)

    def rows_out(s):
        for i in range(1, 16):
            peer = (row + i) % 16
            send(pan.at[s, peer], abuf[s].at[row], a_s.at[s, i], a_r.at[s, i], (peer, col))

    def rows_in(s):
        for i in range(1, 16):
            peer = (row + 16 - i) % 16
            arrived(abuf[s].at[peer], a_s.at[s, i], a_r.at[s, i], (peer, col))

        def take(k, carry):
            block = anc[k, 2 * col + s]
            rows = abuf[s][block].reshape(2, 16, BLK)
            pf[s][0, pl.ds(z, 1), k] = rows[0][None]
            pf[s][1, pl.ds(z, 1), k] = rows[1][None]
            return carry

        lax.fori_loop(0, K, take, 0)
        for h in range(2):
            for d in range(2):
                z_send(s, h, d, 0)

    def hops(h, d):
        return 4 if d == h else 3

    def piece(s, h, d, hop):
        return pf[s].at[h, (z + (8 - hop if d == 0 else hop)) % 8]

    def z_send(s, h, d, hop):
        block = piece(s, h, d, hop)
        send(block, block, z_s.at[s, h, d, hop], z_r.at[s, h, d, hop], z_next[d])

    def ring(s, hop):
        for h in range(2):
            for d in range(2):
                if hop <= hops(h, d):
                    arrived(piece(s, h, d, hop), z_s.at[s, h, d, hop - 1], z_r.at[s, h, d, hop - 1], z_next[d])
                    if hop < hops(h, d):
                        z_send(s, h, d, hop)

    def pair_out(s):
        send(pan.at[s], pbuf.at[s], p_s.at[s], p_r.at[s], x_pair)

    def member(s, block):
        here = jnp.int32(0)
        for k in range(K):
            here = here + (anc[k, 2 * col + s] == block).astype(jnp.int32)
        return here.astype(F32)

    def image(s):
        cacc[...] = jnp.zeros_like(cacc)

        def term(k, carry):
            block = anc[k, 2 * col + s]
            high, low = split(pf[s][:, :, k].reshape(256, BLK))
            for n in range(2):
                s_high, s_low = split(sbuf[((xh + 1 + n) % 2) * NB + block])
                cacc[n] += (
                    jnp.dot(high, s_high, preferred_element_type=F32)
                    + jnp.dot(low, s_high, preferred_element_type=F32)
                    + jnp.dot(high, s_low, preferred_element_type=F32)
                )
            return carry

        lax.fori_loop(0, K, term, 0)
        other = cacc[0] * member(s, 2 * z + 1 - xh)
        cbuf[s] = -other.reshape(2, 8, 16, BLK)
        send(cbuf.at[s], cross.at[s, xh], c_s.at[s], c_r.at[s], x_pair)
        own = cacc[1] * member(s, row)
        cross[s, pl.ds(xh, 1)] = -own.reshape(1, 2, 8, 16, BLK)
        arrived(pbuf.at[s], p_s.at[s], p_r.at[s], x_pair)
        over = (((1,), (1,)), ((), ()))
        product = jnp.zeros((256, W), F32)
        for rows, panel in ((own, pan[s]), (other, pbuf[s])):
            high, low = split(rows)
            p_high, p_low = split(panel.reshape(W, BLK))
            product = product + (
                lax.dot_general(high, p_high, over, preferred_element_type=F32)
                + lax.dot_general(low, p_high, over, preferred_element_type=F32)
                + lax.dot_general(high, p_low, over, preferred_element_type=F32)
            )
        dbuf[s] = product.reshape(2, 8, 16, W)
        for i in (4, 3, 5, 2, 6, 1, 7):
            zz = (z + i) % 8
            send(dbuf.at[s, :, zz], drz.at[s, i], d_s.at[s, i], d_r.at[s, i], at(x, y, zz, core))

    def image_end(s):
        total = diag[s] + dbuf[s, :, pl.ds(z, 1)].reshape(2, 16, W)
        for i in range(1, 8):
            arrived(drz.at[s, i], d_s.at[s, i], d_r.at[s, i], at(x, y, (z + 8 - i) % 8, core))
            total = total + drz[s, i]
        dout[s] = total
        arrived(cross.at[s, 1 - xh], c_s.at[s], c_r.at[s], x_pair)

    sigma_own()
    rows_out(0)
    rows_out(1)
    sigma_x_near()
    rows_in(0)
    sigma_x_far()
    sigma_y_near(0)
    rows_in(1)
    pair_out(0)
    ring(0, 1)
    sigma_y_near(1)
    sigma_y_near(2)
    ring(0, 2)
    ring(1, 1)
    pair_out(1)
    sigma_y_near(3)
    ring(0, 3)
    ring(1, 2)
    sigma_y_far(0)
    sigma_y_far(1)
    ring(0, 4)
    ring(1, 3)
    sigma_y_far(2)
    sigma_y_far(3)
    sigma_other_core()
    image(0)
    ring(1, 4)
    image(1)
    image_end(0)
    image_end(1)
    for copy in sent:
        copy.wait_send()
    block = sigma_at(0, 0, core)
    pltpu.make_async_remote_copy(
        src_ref=block, dst_ref=block, send_sem=sx_s.at[2], recv_sem=sx_r.at[2],
        device_id=x_next[0], device_id_type=MESH,
    ).wait_send()


def local(sigma_anc, panels, diag_blocks, anc_blocks):
    vmem = pl.BlockSpec(memory_space=pltpu.VMEM)
    dma = pltpu.SemaphoreType.DMA
    cross, dout = pl.pallas_call(
        kernel,
        out_shape=(
            jax.ShapeDtypeStruct((2, 2, 2, 8, 16, BLK), F32),
            jax.ShapeDtypeStruct((2, 2, 16, W), F32),
        ),
        in_specs=[pl.BlockSpec(memory_space=pltpu.SMEM), vmem, vmem, vmem],
        out_specs=(vmem, vmem),
        scratch_shapes=[
            pltpu.VMEM((16, 32, BLK), F32),
            pltpu.VMEM((16, 32, BLK), F32),
            pltpu.VMEM((2, 8, K, 16, BLK), F32),
            pltpu.VMEM((2, 8, K, 16, BLK), F32),
            pltpu.VMEM((2 * NB, BLK, BLK), F32),
            pltpu.VMEM((2, 16, 32, BLK), F32),
            pltpu.VMEM((2, 256, BLK), F32),
            pltpu.VMEM((2, 2, 8, 16, BLK), F32),
            pltpu.VMEM((2, 2, 8, 16, W), F32),
            pltpu.VMEM((2, 8, 2, 16, W), F32),
            dma((2, 16)), dma((2, 16)),
            dma((2, 2, 2, 4)), dma((2, 2, 2, 4)),
            dma((2,)), dma((2,)),
            dma((2,)), dma((2,)),
            dma((3,)), dma((3,)),
            dma((4, 3)), dma((4, 3)),
            dma((4, 4)), dma((4, 4)),
            dma((2, 8)), dma((2, 8)),
        ],
        compiler_params=pltpu.CompilerParams(
            collective_id=0, has_side_effects=True, vmem_limit_bytes=56 << 20
        ),
    )(
        anc_blocks.T,
        sigma_anc,
        panels.reshape(2, 16, 32, BLK),
        diag_blocks.reshape(2, 2, 16, W),
    )
    cross = cross.transpose(0, 3, 1, 2, 4, 5)
    return cross.reshape(2 * W, BLK), dout.reshape(2, 32, W)


def solution(mesh):
    placed = (P("prow", "pcol"), P("pcol", "prow"), P("pcol", "prow", None), P())
    return jax.shard_map(
        local,
        mesh=mesh,
        in_specs=placed,
        out_specs=(P("pcol", "prow"), P("pcol", "prow", None)),
        check_vma=False,
    )
```

time: 653 us -> 146 us (0.22)
  the two profiles are of different devices: /device:TPU:8 before, /device:TPU:1 now
where the time goes in v2:
time: 146 us
  Pallas kernels  142 us (97%)
  local copies, waits for them, and re-layouts  3.47 us (2%)
    pallas_call x1, Pallas kernels, local(): pl.pallas_call(kernel, out_shape=(jax.ShapeDtypeStruct((2, 2, 2, 8, 16, B...  142 us

profile of v2, /device:TPU:1, one launch (start us, length us, event | category | flops | bytes accessed | tf_op | source)
XLA Modules:
  0.0 146.1 jit_solution(15537053175800281700)
XLA Ops:
  0.6 142.0 %shard_map.59 = (f32[2,2,2,8,16,384]{5,4,3,2,1,0:T(8,128)}, f32[2,2,16,512]{3,2,1,0:T(8,128)}) custom-call(s32[6,32]{1,0:T(8,128)} %bitcast.11, f32[384,384]{1,0:T(8,128)} %sig.1, f32[2,16,32,384]{3,2,1,0:T(8,128)} %bitcast.6, f32[2,2,16,512]{3,2,1,0:T(8,128)} %bitcast.9), custom_call_target="tpu_custom_call" | custom-call | tf_op jit(solution)/shard_map/pallas_call | solution.py:267
  142.6 0.0 copy-start
  142.6 2.8 %copy.6 = f32[2,8,2,2,16,384]{5,4,3,2,1,0:T(8,128)} copy(f32[2,8,2,2,16,384]{5,4,1,3,2,0:T(8,128)} %bitcast.8) | data formatting | bytes 3145728 | tf_op jit(solution)/shard_map/transpose | solution.py:304
  145.4 0.0 copy-done
  145.4 0.7 copy.8
Async XLA Ops:
  142.6 2.8 %copy-start = (f32[2,2,16,512]{3,2,1,0:T(8,128)S(1)}, f32[2,2,16,512]{3,2,1,0:T(8,128)}, u32[]{:S(2)}) copy-start(f32[2,2,16,512]{3,2,1,0:T(8,128)} %get-tuple-element.5) | copy-start | bytes 393220

commit v3 on v2

--- a/solution.py
+++ b/solution.py
@@ -44,7 +44,7 @@
 
     sbuf[pl.ds(xh * NB + col, 1)] = sig[...].T[None]
     for s in range(2):
-        abuf[s][pl.ds(row, 1)] = pan[s, pl.ds(row, 1)]
+        abuf[s][pl.ds(row, 1)] = pan[s, pl.ds(z, 1), pl.ds(xh, 1)].reshape(1, 32, BLK)
 
     barrier = pltpu.get_barrier_semaphore()
     peers = [((row + i) % 16, col) for i in range(1, 16)] + [*x_next, *y_next, c_pair]
@@ -82,56 +82,71 @@
         for d in range(2):
             send(block, block, sy_s.at[t, d], sy_r.at[t, d], y_next[d])
 
+    def sigma_x(u):
+        block = sigma_at(0, u, core)
+        for d in range(2):
+            send(block, block, sx_s.at[u // 3, d], sx_r.at[u // 3, d], x_next[d])
+
+    def far(block, ssem, rsem, peers, d):
+        @pl.when(core == d)
+        def _():
+            pltpu.make_async_remote_copy(
+                src_ref=block, dst_ref=block, send_sem=ssem, recv_sem=rsem,
+                device_id=peers[d], device_id_type=MESH,
+            ).start()
+
     def sigma_own():
-        block = sigma_at(0, 0, core)
-        for d in range(2):
-            send(block, block, sx_s.at[d], sx_r.at[d], x_next[d])
+        sigma_x(0)
         sigma_y(0)
         sigma_core(0, 0)
 
-    def sigma_x_near():
+    def sigma_x_near(u):
         for d in range(2):
-            block = sigma_at(1 + d, 0, core)
-            arrived(block, sx_s.at[d], sx_r.at[d], x_next[d])
-
-            @pl.when(core == d)
-            def _():
-                pltpu.make_async_remote_copy(
-                    src_ref=block, dst_ref=block, send_sem=sx_s.at[2], recv_sem=sx_r.at[2],
-                    device_id=x_next[d], device_id_type=MESH,
-                ).start()
-
-            sigma_y(1 + d)
-            sigma_core(1 + d, 0)
-
-    def sigma_x_far():
-        block = sigma_at(3, 0, core)
-        arrived(block, sx_s.at[2], sx_r.at[2], x_pair)
-        sigma_y(3)
-        sigma_core(3, 0)
+            block = sigma_at(1 + d, u, core)
+            arrived(block, sx_s.at[u // 3, d], sx_r.at[u // 3, d], x_next[d])
+            far(block, sx_s.at[u // 3, 2], sx_r.at[u // 3, 2], x_next, d)
+            if u == 0:
+                sigma_y(1 + d)
+            sigma_core(1 + d, u)
+
+    def sigma_x_far(u):
+        block = sigma_at(3, u, core)
+        arrived(block, sx_s.at[u // 3, 2], sx_r.at[u // 3, 2], x_pair)
+        if u == 0:
+            sigma_y(3)
+        sigma_core(3, u)
 
     def sigma_y_near(t):
         for d in range(2):
             block = sigma_at(t, 1 + d, core)
             arrived(block, sy_s.at[t, d], sy_r.at[t, d], y_next[d])
-            if d == t % 2:
-                send(block, block, sy_s.at[t, 2], sy_r.at[t, 2], y_next[d])
+            if t == 0:
+                far(block, sy_s.at[0, 2], sy_r.at[0, 2], y_next, d)
             sigma_core(t, 1 + d)
 
-    def sigma_y_far(t):
-        block = sigma_at(t, 3, core)
-        arrived(block, sy_s.at[t, 2], sy_r.at[t, 2], y_next[t % 2])
-        sigma_core(t, 3)
+    def sigma_y_far():
+        block = sigma_at(0, 3, core)
+        arrived(block, sy_s.at[0, 2], sy_r.at[0, 2], y_next[0])
+        sigma_x(3)
+        sigma_core(0, 3)
 
     def sigma_other_core():
         for t in range(4):
             for u in range(4):
                 arrived(sigma_at(t, u, 1 - core), sc_s.at[t, u], sc_r.at[t, u], c_pair)
 
+    def sigma_end():
+        block = sigma_at(0, 0, core)
+        for ssem, rsem in ((sx_s.at[0, 2], sx_r.at[0, 2]), (sx_s.at[1, 2], sx_r.at[1, 2]), (sy_s.at[0, 2], sy_r.at[0, 2])):
+            pltpu.make_async_remote_copy(
+                src_ref=block, dst_ref=block, send_sem=ssem, recv_sem=rsem,
+                device_id=c_pair, device_id_type=MESH,
+            ).wait_send()
+
     def rows_out(s):
         for i in range(1, 16):
             peer = (row + i) % 16
-            send(pan.at[s, peer], abuf[s].at[row], a_s.at[s, i], a_r.at[s, i], (peer, col))
+            send(pan.at[s, peer // 2, peer % 2], abuf[s].at[row], a_s.at[s, i], a_r.at[s, i], (peer, col))
 
     def rows_in(s):
         for i in range(1, 16):
@@ -146,6 +161,8 @@
             return carry
 
         lax.fori_loop(0, K, take, 0)
+
+    def ring_start(s):
         for h in range(2):
             for d in range(2):
                 z_send(s, h, d, 0)
@@ -169,7 +186,7 @@
                         z_send(s, h, d, hop)
 
     def pair_out(s):
-        send(pan.at[s], pbuf.at[s], p_s.at[s], p_r.at[s], x_pair)
+        send(pan.at[s, :, xh], pbuf.at[s, :, xh], p_s.at[s], p_r.at[s], x_pair)
 
     def member(s, block):
         here = jnp.int32(0)
@@ -198,7 +215,12 @@
         send(cbuf.at[s], cross.at[s, xh], c_s.at[s], c_r.at[s], x_pair)
         own = cacc[1] * member(s, row)
         cross[s, pl.ds(xh, 1)] = -own.reshape(1, 2, 8, 16, BLK)
-        arrived(pbuf.at[s], p_s.at[s], p_r.at[s], x_pair)
+        mine = jnp.zeros((2, 8, 16, BLK), F32)
+        for k in range(K):
+            mine = mine + pf[s][:, :, k] * (anc[k, 2 * col + s] == 2 * z + 1 - xh).astype(F32)
+        for h in range(2):
+            pbuf[s, :, pl.ds(xh, 1), 16 * h : 16 * h + 16] = mine[h].reshape(8, 1, 16, BLK)
+        arrived(pbuf.at[s, :, 1 - xh], p_s.at[s], p_r.at[s], x_pair)
         over = (((1,), (1,)), ((), ()))
         product = jnp.zeros((256, W), F32)
         for rows, panel in ((own, pan[s]), (other, pbuf[s])):
@@ -225,40 +247,37 @@
     sigma_own()
     rows_out(0)
     rows_out(1)
-    sigma_x_near()
+    sigma_y_near(0)
+    sigma_x_near(0)
     rows_in(0)
-    sigma_x_far()
-    sigma_y_near(0)
+    ring_start(0)
+    sigma_x_far(0)
+    sigma_y_far()
+    sigma_y_near(1)
     rows_in(1)
-    pair_out(0)
     ring(0, 1)
-    sigma_y_near(1)
+    ring_start(1)
+    sigma_x_near(3)
     sigma_y_near(2)
     ring(0, 2)
+    sigma_x_far(3)
+    pair_out(0)
+    ring(0, 3)
     ring(1, 1)
+    sigma_y_near(3)
+    ring(0, 4)
+    ring(1, 2)
+    sigma_other_core()
     pair_out(1)
-    sigma_y_near(3)
-    ring(0, 3)
-    ring(1, 2)
-    sigma_y_far(0)
-    sigma_y_far(1)
-    ring(0, 4)
+    image(0)
     ring(1, 3)
-    sigma_y_far(2)
-    sigma_y_far(3)
-    sigma_other_core()
-    image(0)
     ring(1, 4)
     image(1)
     image_end(0)
     image_end(1)
     for copy in sent:
         copy.wait_send()
-    block = sigma_at(0, 0, core)
-    pltpu.make_async_remote_copy(
-        src_ref=block, dst_ref=block, send_sem=sx_s.at[2], recv_sem=sx_r.at[2],
-        device_id=x_next[0], device_id_type=MESH,
-    ).wait_send()
+    sigma_end()
 
 
 def local(sigma_anc, panels, diag_blocks, anc_blocks):
@@ -278,7 +297,7 @@
             pltpu.VMEM((2, 8, K, 16, BLK), F32),
             pltpu.VMEM((2, 8, K, 16, BLK), F32),
             pltpu.VMEM((2 * NB, BLK, BLK), F32),
-            pltpu.VMEM((2, 16, 32, BLK), F32),
+            pltpu.VMEM((2, 8, 2, 32, BLK), F32),
             pltpu.VMEM((2, 256, BLK), F32),
             pltpu.VMEM((2, 2, 8, 16, BLK), F32),
             pltpu.VMEM((2, 2, 8, 16, W), F32),
@@ -287,7 +306,7 @@
             dma((2, 2, 2, 4)), dma((2, 2, 2, 4)),
             dma((2,)), dma((2,)),
             dma((2,)), dma((2,)),
-            dma((3,)), dma((3,)),
+            dma((2, 3)), dma((2, 3)),
             dma((4, 3)), dma((4, 3)),
             dma((4, 4)), dma((4, 4)),
             dma((2, 8)), dma((2, 8)),
@@ -298,7 +317,7 @@
     )(
         anc_blocks.T,
         sigma_anc,
-        panels.reshape(2, 16, 32, BLK),
+        panels.reshape(2, 8, 2, 32, BLK),
         diag_blocks.reshape(2, 2, 16, W),
     )
     cross = cross.transpose(0, 3, 1, 2, 4, 5)

time: 146 us -> 134 us (0.918)
  the two profiles are of different devices: /device:TPU:1 before, /device:TPU:8 now
where the time goes in v3:
time: 134 us; the launch traced here: 132 us
  Pallas kernels  127 us (95%)
  local copies, waits for them, and re-layouts  3.47 us (3%)
    pallas_call x1, Pallas kernels, local(): pl.pallas_call(kernel, out_shape=(jax.ShapeDtypeStruct((2, 2, 2, 8, 16, B...  127 us
    transpose x1, local copies, waits for them, and re-layouts, local(): cross = cross.transpose(0, 3, 1, 2, 4, 5)  2.81 us

profile of v3, /device:TPU:8, one launch (start us, length us, event | category | flops | bytes accessed | tf_op | source)
XLA Modules:
  0.0 131.6 jit_solution(367712503017256947)
XLA Ops:
  0.6 127.4 %shard_map.59 = (f32[2,2,2,8,16,384]{5,4,3,2,1,0:T(8,128)}, f32[2,2,16,512]{3,2,1,0:T(8,128)}) custom-call(s32[6,32]{1,0:T(8,128)} %bitcast.11, f32[384,384]{1,0:T(8,128)} %sig.1, f32[2,8,2,32,384]{4,3,2,1,0:T(8,128)} %bitcast.6, f32[2,2,16,512]{3,2,1,0:T(8,128)} %bitcast.9), custom_call_target="tpu_custom_call" | custom-call | tf_op jit(solution)/shard_map/pallas_call | solution.py:286
  128.1 0.0 copy-start
  128.1 2.8 %copy.6 = f32[2,8,2,2,16,384]{5,4,3,2,1,0:T(8,128)} copy(f32[2,8,2,2,16,384]{5,4,1,3,2,0:T(8,128)} %bitcast.8) | data formatting | bytes 3145728 | tf_op jit(solution)/shard_map/transpose | solution.py:323
  130.9 0.0 copy-done
  130.9 0.7 copy.8
Async XLA Ops:
  128.1 2.8 %copy-start = (f32[2,2,16,512]{3,2,1,0:T(8,128)S(1)}, f32[2,2,16,512]{3,2,1,0:T(8,128)}, u32[]{:S(2)}) copy-start(f32[2,2,16,512]{3,2,1,0:T(8,128)} %get-tuple-element.5) | copy-start | bytes 393220

commit v4 on v3

--- a/solution.py
+++ b/solution.py
@@ -21,7 +21,7 @@
 
 def kernel(
     anc, sig, pan, diag, cross, dout,
-    abuf0, abuf1, pf0, pf1, sbuf, pbuf, cacc, cbuf, dbuf, drz,
+    abuf0, abuf1, pf0, pf1, s_own, s_oth, pbuf, cacc, cbuf, dbuf, drz,
     a_s, a_r, z_s, z_r, p_s, p_r, c_s, c_r, sx_s, sx_r, sy_s, sy_r, sc_s, sc_r, d_s, d_r,
 ):
     row, col = lax.axis_index("prow"), lax.axis_index("pcol")
@@ -33,16 +33,14 @@
     def at(xx, yy, zz, cc):
         return (zz * 2 + xx // 2, ((xx % 2) * 4 + yy) * 2 + cc)
 
-    def sigma_block(xx, yy, cc):
-        return sbuf.at[(xx // 2) * NB + ((xx % 2) * 4 + yy) * 2 + cc]
-
-    x_next = (at((x + 1) % 4, y, z, core), at((x + 3) % 4, y, z, core))
+    x_same, x_cross = (x + 1 + 2 * xl) % 4, (x + 3 + 2 * xl) % 4
+    x_next = (at(x_same, y, z, core), at(x_cross, y, z, core))
     y_next = (at(x, (y + 1) % 4, z, core), at(x, (y + 3) % 4, z, core))
     z_next = (at(x, y, (z + 1) % 8, core), at(x, y, (z + 7) % 8, core))
     x_pair = at((x + 2) % 4, y, z, core)
     c_pair = at(x, y, z, 1 - core)
 
-    sbuf[pl.ds(xh * NB + col, 1)] = sig[...].T[None]
+    s_own[pl.ds(col, 1)] = sig[...].T[None]
     for s in range(2):
         abuf[s][pl.ds(row, 1)] = pan[s, pl.ds(z, 1), pl.ds(xh, 1)].reshape(1, 32, BLK)
 
@@ -68,10 +66,11 @@
             device_id=peer, device_id_type=MESH,
         ).wait_recv()
 
-    steps = (0, 3, 1, 2)
-
-    def sigma_at(t, u, cc):
-        return sigma_block((x + steps[t]) % 4, (y + steps[u]) % 4, cc)
+    def sigma_at(t, u, cc, owner=None):
+        xx = (x, x_same, x_cross, (x + 2) % 4)[t]
+        yy = (y + (0, 3, 1, 2)[u]) % 4
+        owner = t < 2 if owner is None else owner
+        return (s_own if owner else s_oth).at[((xx % 2) * 4 + yy) * 2 + cc]
 
     def sigma_core(t, u):
         block = sigma_at(t, u, core)
@@ -83,19 +82,18 @@
             send(block, block, sy_s.at[t, d], sy_r.at[t, d], y_next[d])
 
     def sigma_x(u):
-        block = sigma_at(0, u, core)
         for d in range(2):
-            send(block, block, sx_s.at[u // 3, d], sx_r.at[u // 3, d], x_next[d])
-
-    def far(block, ssem, rsem, peers, d):
+            send(sigma_at(0, u, core), sigma_at(0, u, core, d == 0), sx_s.at[u // 3, d], sx_r.at[u // 3, d], x_next[d])
+
+    def far(src, dst, ssem, rsem, peer, d):
         @pl.when(core == d)
         def _():
             pltpu.make_async_remote_copy(
-                src_ref=block, dst_ref=block, send_sem=ssem, recv_sem=rsem,
-                device_id=peers[d], device_id_type=MESH,
+                src_ref=src, dst_ref=dst, send_sem=ssem, recv_sem=rsem,
+                device_id=peer, device_id_type=MESH,
             ).start()
 
-    def sigma_own():
+    def sigma_first():
         sigma_x(0)
         sigma_y(0)
         sigma_core(0, 0)
@@ -104,7 +102,7 @@
         for d in range(2):
             block = sigma_at(1 + d, u, core)
             arrived(block, sx_s.at[u // 3, d], sx_r.at[u // 3, d], x_next[d])
-            far(block, sx_s.at[u // 3, 2], sx_r.at[u // 3, 2], x_next, d)
+            far(block, sigma_at(1 + d, u, core, False), sx_s.at[u // 3, 2], sx_r.at[u // 3, 2], x_next[1 - d], d)
             if u == 0:
                 sigma_y(1 + d)
             sigma_core(1 + d, u)
@@ -121,7 +119,7 @@
             block = sigma_at(t, 1 + d, core)
             arrived(block, sy_s.at[t, d], sy_r.at[t, d], y_next[d])
             if t == 0:
-                far(block, sy_s.at[0, 2], sy_r.at[0, 2], y_next, d)
+                far(block, block, sy_s.at[0, 2], sy_r.at[0, 2], y_next[d], d)
             sigma_core(t, 1 + d)
 
     def sigma_y_far():
@@ -130,8 +128,8 @@
         sigma_x(3)
         sigma_core(0, 3)
 
-    def sigma_other_core():
-        for t in range(4):
+    def sigma_ready(n):
+        for t in ((2, 3), (0, 1))[n]:
             for u in range(4):
                 arrived(sigma_at(t, u, 1 - core), sc_s.at[t, u], sc_r.at[t, u], c_pair)
 
@@ -144,7 +142,7 @@
             ).wait_send()
 
     def rows_out(s):
-        for i in range(1, 16):
+        for i in (8, 6, 10, 4, 12, 2, 14, 7, 9, 5, 11, 3, 13, 1, 15):
             peer = (row + i) % 16
             send(pan.at[s, peer // 2, peer % 2], abuf[s].at[row], a_s.at[s, i], a_r.at[s, i], (peer, col))
 
@@ -195,26 +193,36 @@
         return here.astype(F32)
 
     def image(s):
-        cacc[...] = jnp.zeros_like(cacc)
-
         def term(k, carry):
-            block = anc[k, 2 * col + s]
-            high, low = split(pf[s][:, :, k].reshape(256, BLK))
+            high, low, s_high, s_low = [], [], [], []
+            for i in range(2):
+                block = anc[2 * k + i, 2 * col + s]
+                p_high, p_low = split(pf[s][:, :, 2 * k + i].reshape(256, BLK))
+                high.append(p_high)
+                low.append(p_low)
+                for rows in (s_oth, s_own):
+                    r_high, r_low = split(rows[block])
+                    s_high.append(r_high)
+                    s_low.append(r_low)
+            left = jnp.concatenate(high + low + high, axis=1)
+            right = jnp.concatenate(
+                [jnp.concatenate(s_high[n::2] + s_high[n::2] + s_low[n::2], axis=0) for n in range(2)], axis=1
+            )
+            part = jnp.dot(left, right, preferred_element_type=F32)
             for n in range(2):
-                s_high, s_low = split(sbuf[((xh + 1 + n) % 2) * NB + block])
-                cacc[n] += (
-                    jnp.dot(high, s_high, preferred_element_type=F32)
-                    + jnp.dot(low, s_high, preferred_element_type=F32)
-                    + jnp.dot(high, s_low, preferred_element_type=F32)
-                )
+                cacc[n] = jnp.where(k == 0, 0.0, cacc[n]) + part[:, n * BLK : (n + 1) * BLK]
             return carry
 
-        lax.fori_loop(0, K, term, 0)
+        lax.fori_loop(0, K // 2, term, 0)
         other = cacc[0] * member(s, 2 * z + 1 - xh)
+        cacc[0] = other
         cbuf[s] = -other.reshape(2, 8, 16, BLK)
         send(cbuf.at[s], cross.at[s, xh], c_s.at[s], c_r.at[s], x_pair)
         own = cacc[1] * member(s, row)
+        cacc[1] = own
         cross[s, pl.ds(xh, 1)] = -own.reshape(1, 2, 8, 16, BLK)
+
+    def image_out(s):
         mine = jnp.zeros((2, 8, 16, BLK), F32)
         for k in range(K):
             mine = mine + pf[s][:, :, k] * (anc[k, 2 * col + s] == 2 * z + 1 - xh).astype(F32)
@@ -222,29 +230,44 @@
             pbuf[s, :, pl.ds(xh, 1), 16 * h : 16 * h + 16] = mine[h].reshape(8, 1, 16, BLK)
         arrived(pbuf.at[s, :, 1 - xh], p_s.at[s], p_r.at[s], x_pair)
         over = (((1,), (1,)), ((), ()))
-        product = jnp.zeros((256, W), F32)
-        for rows, panel in ((own, pan[s]), (other, pbuf[s])):
+        left, right = [], []
+        for rows, panel in ((cacc[1], pan[s]), (cacc[0], pbuf[s])):
             high, low = split(rows)
             p_high, p_low = split(panel.reshape(W, BLK))
-            product = product + (
-                lax.dot_general(high, p_high, over, preferred_element_type=F32)
-                + lax.dot_general(low, p_high, over, preferred_element_type=F32)
-                + lax.dot_general(high, p_low, over, preferred_element_type=F32)
-            )
+            left += [high, low, high]
+            right += [p_high, p_high, p_low]
+        product = lax.dot_general(
+            jnp.concatenate(left, axis=1), jnp.concatenate(right, axis=1),
+            (((1,), (1,)), ((), ())), preferred_element_type=F32,
+        )
         dbuf[s] = product.reshape(2, 8, 16, W)
-        for i in (4, 3, 5, 2, 6, 1, 7):
-            zz = (z + i) % 8
-            send(dbuf.at[s, :, zz], drz.at[s, i], d_s.at[s, i], d_r.at[s, i], at(x, y, zz, core))
-
-    def image_end(s):
-        total = diag[s] + dbuf[s, :, pl.ds(z, 1)].reshape(2, 16, W)
-        for i in range(1, 8):
-            arrived(drz.at[s, i], d_s.at[s, i], d_r.at[s, i], at(x, y, (z + 8 - i) % 8, core))
-            total = total + drz[s, i]
-        dout[s] = total
+        sums(s, 0)
+
+    def sums(s, hop):
+        for h in range(2):
+            for d in range(2):
+                if hop >= hops(h, d):
+                    continue
+                away = hops(h, d) - hop
+                own = dbuf.at[s, h, (z + (away if d == 0 else 8 - away)) % 8]
+                if hop > 0:
+                    slot = drz.at[s, h, d, hop - 1]
+                    arrived(slot, d_s.at[s, h, d, hop - 1], d_r.at[s, h, d, hop - 1], z_next[d])
+                    slot[...] += own[...]
+                    own = slot
+                send(own, drz.at[s, h, d, hop], d_s.at[s, h, d, hop], d_r.at[s, h, d, hop], z_next[d])
+
+    def sums_end(s):
+        for h in range(2):
+            total = diag[s, h] + dbuf[s, h, pl.ds(z, 1)].reshape(16, W)
+            for d in range(2):
+                hop = hops(h, d) - 1
+                arrived(drz.at[s, h, d, hop], d_s.at[s, h, d, hop], d_r.at[s, h, d, hop], z_next[d])
+                total = total + drz[s, h, d, hop]
+            dout[s, h] = total
         arrived(cross.at[s, 1 - xh], c_s.at[s], c_r.at[s], x_pair)
 
-    sigma_own()
+    sigma_first()
     rows_out(0)
     rows_out(1)
     sigma_y_near(0)
@@ -253,28 +276,37 @@
     ring_start(0)
     sigma_x_far(0)
     sigma_y_far()
+    rows_in(1)
+    ring_start(1)
+    ring(0,1)
     sigma_y_near(1)
-    rows_in(1)
-    ring(0, 1)
-    ring_start(1)
+    ring(1,1)
     sigma_x_near(3)
+    ring(0,2)
     sigma_y_near(2)
-    ring(0, 2)
+    ring(1,2)
     sigma_x_far(3)
     pair_out(0)
-    ring(0, 3)
-    ring(1, 1)
+    ring(0,3)
     sigma_y_near(3)
-    ring(0, 4)
-    ring(1, 2)
-    sigma_other_core()
+    ring(1,3)
     pair_out(1)
+    ring(0,4)
+    sigma_ready(1)
+    sigma_ready(0)
     image(0)
-    ring(1, 3)
-    ring(1, 4)
+    image_out(0)
+    ring(1,4)
     image(1)
-    image_end(0)
-    image_end(1)
+    sums(0,1)
+    image_out(1)
+    sums(0,2)
+    sums(1,1)
+    sums(0,3)
+    sums(1,2)
+    sums(1,3)
+    sums_end(0)
+    sums_end(1)
     for copy in sent:
         copy.wait_send()
     sigma_end()
@@ -296,12 +328,13 @@
             pltpu.VMEM((16, 32, BLK), F32),
             pltpu.VMEM((2, 8, K, 16, BLK), F32),
             pltpu.VMEM((2, 8, K, 16, BLK), F32),
-            pltpu.VMEM((2 * NB, BLK, BLK), F32),
+            pltpu.VMEM((NB, BLK, BLK), F32),
+            pltpu.VMEM((NB, BLK, BLK), F32),
             pltpu.VMEM((2, 8, 2, 32, BLK), F32),
             pltpu.VMEM((2, 256, BLK), F32),
             pltpu.VMEM((2, 2, 8, 16, BLK), F32),
             pltpu.VMEM((2, 2, 8, 16, W), F32),
-            pltpu.VMEM((2, 8, 2, 16, W), F32),
+            pltpu.VMEM((2, 2, 2, 4, 16, W), F32),
             dma((2, 16)), dma((2, 16)),
             dma((2, 2, 2, 4)), dma((2, 2, 2, 4)),
             dma((2,)), dma((2,)),
@@ -309,7 +342,7 @@
             dma((2, 3)), dma((2, 3)),
             dma((4, 3)), dma((4, 3)),
             dma((4, 4)), dma((4, 4)),
-            dma((2, 8)), dma((2, 8)),
+            dma((2, 2, 2, 4)), dma((2, 2, 2, 4)),
         ],
         compiler_params=pltpu.CompilerParams(
             collective_id=0, has_side_effects=True, vmem_limit_bytes=56 << 20

time: 134 us -> 121 us (0.903)
  Pallas kernels: 127 us -> 115 us
    pallas_call x1, Pallas kernels: 127 us -> 115 us  [local(): pl.pallas_call(kernel, out_shape=(jax.ShapeDtypeStruct((2, 2, 2, 8, 16, B...]
where the time goes in v4:
time: 121 us; the launch traced here: 119 us
  Pallas kernels  115 us (95%)
  local copies, waits for them, and re-layouts  3.47 us (3%)
    pallas_call x1, Pallas kernels, local(): pl.pallas_call(kernel, out_shape=(jax.ShapeDtypeStruct((2, 2, 2, 8, 16, B...  115 us
    transpose x1, local copies, waits for them, and re-layouts, local(): cross = cross.transpose(0, 3, 1, 2, 4, 5)  2.81 us

profile of v4, /device:TPU:8, one launch (start us, length us, event | category | flops | bytes accessed | tf_op | source)
XLA Modules:
  0.0 119.2 jit_solution(8493280121118853674)
XLA Ops:
  0.6 115.1 %shard_map.59 = (f32[2,2,2,8,16,384]{5,4,3,2,1,0:T(8,128)}, f32[2,2,16,512]{3,2,1,0:T(8,128)}) custom-call(s32[6,32]{1,0:T(8,128)} %bitcast.11, f32[384,384]{1,0:T(8,128)} %sig.1, f32[2,8,2,32,384]{4,3,2,1,0:T(8,128)} %bitcast.6, f32[2,2,16,512]{3,2,1,0:T(8,128)} %bitcast.9), custom_call_target="tpu_custom_call" | custom-call | tf_op jit(solution)/shard_map/pallas_call | solution.py:318
  115.7 0.0 copy-start
  115.7 2.8 %copy.6 = f32[2,8,2,2,16,384]{5,4,3,2,1,0:T(8,128)} copy(f32[2,8,2,2,16,384]{5,4,1,3,2,0:T(8,128)} %bitcast.8) | data formatting | bytes 3145728 | tf_op jit(solution)/shard_map/transpose | solution.py:356
  118.6 0.0 copy-done
  118.6 0.7 copy.8
Async XLA Ops:
  115.7 2.8 %copy-start = (f32[2,2,16,512]{3,2,1,0:T(8,128)S(1)}, f32[2,2,16,512]{3,2,1,0:T(8,128)}, u32[]{:S(2)}) copy-start(f32[2,2,16,512]{3,2,1,0:T(8,128)} %get-tuple-element.5) | copy-start | bytes 393220

commit v5 on v4

--- a/solution.py
+++ b/solution.py
@@ -21,7 +21,7 @@
 
 def kernel(
     anc, sig, pan, diag, cross, dout,
-    abuf0, abuf1, pf0, pf1, s_own, s_oth, pbuf, cacc, cbuf, dbuf, drz,
+    abuf0, abuf1, pf0, pf1, s_own, s_oth, pbuf, cacc, cbuf, dbuf, drz, p_hi, p_lo,
     a_s, a_r, z_s, z_r, p_s, p_r, c_s, c_r, sx_s, sx_r, sy_s, sy_r, sc_s, sc_r, d_s, d_r,
 ):
     row, col = lax.axis_index("prow"), lax.axis_index("pcol")
@@ -43,6 +43,9 @@
     s_own[pl.ds(col, 1)] = sig[...].T[None]
     for s in range(2):
         abuf[s][pl.ds(row, 1)] = pan[s, pl.ds(z, 1), pl.ds(xh, 1)].reshape(1, 32, BLK)
+
+    for s in range(2):
+        p_hi[s], p_lo[s] = split(pan[s].reshape(W, BLK))
 
     barrier = pltpu.get_barrier_semaphore()
     peers = [((row + i) % 16, col) for i in range(1, 16)] + [*x_next, *y_next, c_pair]
@@ -231,9 +234,9 @@
         arrived(pbuf.at[s, :, 1 - xh], p_s.at[s], p_r.at[s], x_pair)
         over = (((1,), (1,)), ((), ()))
         left, right = [], []
-        for rows, panel in ((cacc[1], pan[s]), (cacc[0], pbuf[s])):
+        for rows, parts in ((cacc[1], (p_hi[s], p_lo[s])), (cacc[0], split(pbuf[s].reshape(W, BLK)))):
             high, low = split(rows)
-            p_high, p_low = split(panel.reshape(W, BLK))
+            p_high, p_low = parts
             left += [high, low, high]
             right += [p_high, p_high, p_low]
         product = lax.dot_general(
@@ -335,6 +338,8 @@
             pltpu.VMEM((2, 2, 8, 16, BLK), F32),
             pltpu.VMEM((2, 2, 8, 16, W), F32),
             pltpu.VMEM((2, 2, 2, 4, 16, W), F32),
+            pltpu.VMEM((2, W, BLK), BF16),
+            pltpu.VMEM((2, W, BLK), BF16),
             dma((2, 16)), dma((2, 16)),
             dma((2, 2, 2, 4)), dma((2, 2, 2, 4)),
             dma((2,)), dma((2,)),

time: 121 us -> 121 us (level)
  no operation moved by 1% of the time
where the time goes in v5:
time: 121 us; the launch traced here: 120 us
  Pallas kernels  115 us (95%)
  local copies, waits for them, and re-layouts  3.47 us (3%)
    pallas_call x1, Pallas kernels, local(): pl.pallas_call(kernel, out_shape=(jax.ShapeDtypeStruct((2, 2, 2, 8, 16, B...  115 us
    transpose x1, local copies, waits for them, and re-layouts, local(): cross = cross.transpose(0, 3, 1, 2, 4, 5)  2.81 us

profile of v5, /device:TPU:8, one launch (start us, length us, event | category | flops | bytes accessed | tf_op | source)
XLA Modules:
  0.0 119.6 jit_solution(12159779468718948730)
XLA Ops:
  0.6 115.4 %shard_map.59 = (f32[2,2,2,8,16,384]{5,4,3,2,1,0:T(8,128)}, f32[2,2,16,512]{3,2,1,0:T(8,128)}) custom-call(s32[6,32]{1,0:T(8,128)} %bitcast.11, f32[384,384]{1,0:T(8,128)} %sig.1, f32[2,8,2,32,384]{4,3,2,1,0:T(8,128)} %bitcast.6, f32[2,2,16,512]{3,2,1,0:T(8,128)} %bitcast.9), custom_call_target="tpu_custom_call" | custom-call | tf_op jit(solution)/shard_map/pallas_call | solution.py:321
  116.1 0.0 copy-start
  116.1 2.8 %copy.6 = f32[2,8,2,2,16,384]{5,4,3,2,1,0:T(8,128)} copy(f32[2,8,2,2,16,384]{5,4,1,3,2,0:T(8,128)} %bitcast.8) | data formatting | bytes 3145728 | tf_op jit(solution)/shard_map/transpose | solution.py:361
  118.9 0.0 copy-done
  118.9 0.7 copy.8
Async XLA Ops:
  116.1 2.8 %copy-start = (f32[2,2,16,512]{3,2,1,0:T(8,128)S(1)}, f32[2,2,16,512]{3,2,1,0:T(8,128)}, u32[]{:S(2)}) copy-start(f32[2,2,16,512]{3,2,1,0:T(8,128)} %get-tuple-element.5) | copy-start | bytes 393220
